TPU v7x, 512 devices: a whole 4x4x16 slice. The times are simulated.
512 devices in a mesh: alt: 8 (over x, y_hi), strip: 64 (over z, y_lo, core).
Axes of the slice: x: 4, y: 4 (y_hi: 2, y_lo: 2; y = y_hi * 2 + y_lo), z: 16, core: 2. Of those that a mesh axis runs over, the one named last changes fastest.
Arguments:
- screens: bfloat16 [16, 512, 512], P('alt', 'strip'), may hold values from -2.390625 to 2.390625
- row_offset: int32 [2, 16, 2], replicated, may hold values from 0 to 341, as said below
- col_offset: int32 [2, 16, 2], replicated, may hold values from 0 to 341, as said below
- layer_bin: int32 [16], replicated, may hold values from 0 to 15
- illumination: float32 [16, 12800], P(None, ('alt', 'strip')), may hold values from 0.3 to 1
- reconstructor: bfloat16 [2, 12800, 6000], P(None, ('alt', 'strip')), may hold values from -0.0390625 to 0.0390625
- sat_code: int32 [6000], replicated, may hold values from 1 to 16
Outputs:
- slopes: float32 [2, 2, 12800], P(None, None, ('alt', 'strip'))
- commands: float32 [2, 6000], replicated
Inputs may be any that keep to these rules, and one draw needn't show every extreme that they name: Every footprint lies inside the screen: row_offset[f, l, g] + (319) shrink_l <= 511. Every footprint lies inside the screen: col_offset[f, l, g] + (319) shrink_l <= 511.
All inputs are finite; a program needn't handle non-finite values.
Results may differ from a plain program's by a relative error of at most 0.0028.
Values sent between devices are 32-bit elements; how exact they have to be, the bound alone decides.
No kernel may reach another device: no remote copies, remote signals or barrier semaphores. Data moves between devices by JAX's collectives and lax.ppermute only.
A program may use at most 64 MiB of HBM per device.

v0:
```python
import math
import jax
import jax.numpy as jnp
from jax import lax
from jax.sharding import PartitionSpec as P

LENSLETS = 80
PIXELS = 4
GUIDE_STARS = 2
FRAMES = 2
ACTUATORS = 6000
PUPIL_PIX = 320
WINDOW = 384
SUBAPS_ALL = 12800
highest = lax.Precision.HIGHEST
loop_gain = 0.5
code_step = 0.125
bin_step = 0.03125


def bilinear(offsets):
    return jnp.maximum(0.0, 1.0 - jnp.abs(offsets))


def dft_tables():
    padded = 2 * PIXELS
    freq_index = jnp.arange(padded * padded, dtype=jnp.int32)
    freq_row = freq_index // padded
    freq_col = freq_index % padded
    pix_index = jnp.arange(PIXELS * PIXELS, dtype=jnp.int32)
    pix_row = pix_index // PIXELS
    pix_col = pix_index % PIXELS
    turn_count = (
        freq_row[:, None] * pix_row[None, :] + freq_col[:, None] * pix_col[None, :]
    ) % padded
    angles = turn_count.astype(jnp.float32) * (2.0 * math.pi / padded)
    coord_row = ((freq_row + PIXELS) % padded - PIXELS).astype(jnp.float32)
    coord_col = ((freq_col + PIXELS) % padded - PIXELS).astype(jnp.float32)
    return (jnp.cos(angles), jnp.sin(angles), coord_row, coord_col)


def centroids(pupil_phase, illumination, tables):
    cosine, sine_table, coord_row, coord_col = tables
    field_re = illumination * jnp.cos(pupil_phase)
    field_im = illumination * jnp.sin(pupil_phase)
    real_part = jnp.dot(cosine, field_re, precision=highest) + jnp.dot(
        sine_table, field_im, precision=highest
    )
    imag_part = jnp.dot(cosine, field_im, precision=highest) - jnp.dot(
        sine_table, field_re, precision=highest
    )
    intensity = real_part * real_part + imag_part * imag_part
    flux_sum = jnp.sum(intensity, axis=0)
    slope_row = jnp.sum(intensity * coord_row[:, None], axis=0) / flux_sum
    slope_col = jnp.sum(intensity * coord_col[:, None], axis=0) / flux_sum
    return jnp.stack([slope_row, slope_col])


def shards(screens, row_offset, col_offset, layer_bin, illumination, reconstructor, sat_code):
    layer_dev = screens.shape[0]
    rows_here = screens.shape[1]
    count_here = illumination.shape[1]
    group_pos = lax.axis_index("alt")
    strip_pos = lax.axis_index("strip")
    row_global = strip_pos * rows_here + jnp.arange(rows_here, dtype=jnp.int32)
    pupil_idx = jnp.arange(PUPIL_PIX, dtype=jnp.float32)
    window_idx = jnp.arange(WINDOW, dtype=jnp.float32)
    widened_layers = [
        jnp.pad(screens[layer_no], ((0, 0), (0, WINDOW))) for layer_no in range(layer_dev)
    ]
    frame_terms = []
    for frame_no in range(FRAMES):
        running = jnp.zeros((PIXELS, PIXELS, GUIDE_STARS, LENSLETS, LENSLETS), jnp.float32)
        for layer_no in range(layer_dev):
            layer_pos = group_pos * layer_dev + layer_no
            tops = lax.dynamic_index_in_dim(row_offset[frame_no], layer_pos, 0, keepdims=False)
            lefts = lax.dynamic_index_in_dim(col_offset[frame_no], layer_pos, 0, keepdims=False)
            bin_value = lax.dynamic_index_in_dim(layer_bin, layer_pos, 0, keepdims=False)
            shrink = 1.0 - bin_value.astype(jnp.float32) * bin_step
            col_weights = bilinear(window_idx[None, :] - pupil_idx[:, None] * shrink)
            widened = widened_layers[layer_no]

            def cut_columns(left_col):
                return lax.dynamic_slice_in_dim(widened, left_col, WINDOW, 1)

            strips = jax.vmap(cut_columns)(lefts).astype(jnp.float32)
            across = jnp.einsum("drc,jc->drj", strips, col_weights, precision=highest)
            offsets = (row_global[None, :] - tops[:, None]).astype(jnp.float32)
            row_weights = bilinear(offsets[:, None, :] - pupil_idx[None, :, None] * shrink)
            running = running + jnp.einsum(
                "dapr,drbq->pqdab",
                row_weights.reshape(GUIDE_STARS, LENSLETS, PIXELS, rows_here),
                across.reshape(GUIDE_STARS, rows_here, LENSLETS, PIXELS),
                precision=highest,
            )
        frame_terms.append(running.reshape(PIXELS * PIXELS, SUBAPS_ALL))
    phase_terms = jnp.concatenate(frame_terms, axis=0)
    owned = lax.psum_scatter(phase_terms, ("alt", "strip"), scatter_dimension=1, tiled=True)
    pupil_phase = owned.reshape(FRAMES, PIXELS * PIXELS, count_here)
    tables = dft_tables()
    slopes = jnp.stack(
        [centroids(pupil_phase[frame_no], illumination, tables) for frame_no in range(FRAMES)]
    )
    rounded = slopes.astype(jnp.bfloat16).reshape(FRAMES, 2 * count_here)
    partial_value = jnp.dot(
        rounded,
        reconstructor.reshape(2 * count_here, ACTUATORS),
        preferred_element_type=jnp.float32,
    )
    updates = lax.psum(partial_value, ("alt", "strip"))
    limits = sat_code.astype(jnp.float32) * code_step
    first_cmd = jnp.clip(loop_gain * updates[0], -limits, limits)
    second_cmd = jnp.clip(first_cmd + loop_gain * updates[1], -limits, limits)
    return (slopes, jnp.stack([first_cmd, second_cmd]))


def solution(mesh):
    placed = (
        P("alt", "strip", None),
        P(),
        P(),
        P(),
        P(None, ("alt", "strip")),
        P(None, ("alt", "strip"), None),
        P(),
    )
    return jax.shard_map(
        shards,
        mesh=mesh,
        in_specs=placed,
        out_specs=(P(None, None, ("alt", "strip")), P()),
        check_vma=False,
    )
```

profile of v0, /device:TPU:1, one launch (start us, length us, event | category | flops | bytes accessed | tf_op | source)
XLA Modules:
  0.0 635.3 jit_solution(2373824298019678638)
XLA Ops:
  7.2 1.4 fusion.161
  10.0 0.7 fusion.159
  10.8 0.7 fusion.160
  11.8 0.7 slice_bitcast_fusion
  12.6 2.7 while.4
  13.2 0.7 bitcast_dynamic-update-slice_fusion.8
  14.6 0.7 bitcast_dynamic-update-slice_fusion.8
  15.5 2.5 while.5
  19.2 1.2 fusion.21
  20.5 1.2 fusion.1
  22.1 1.7 reshape.445
  24.2 2.7 while.6
  24.8 0.7 bitcast_dynamic-update-slice_fusion.10
  26.2 0.7 bitcast_dynamic-update-slice_fusion.10
  27.6 2.6 while.7
  28.2 0.7 bitcast_dynamic-update-slice_fusion.11
  29.5 0.7 bitcast_dynamic-update-slice_fusion.11
  30.8 1.2 fusion.18
  32.0 1.2 fusion
  33.7 1.7 reshape.448
  35.4 2.5 pad_maximum_fusion
  38.0 477.4 %all-reduce.9.cloned.1.call-done = f32[32,12800]{1,0:T(8,128)} async-done(((f32[32,12800]{1,0:T(8,128)}), f32[32,12800]{1,0:T(8,128)}) %all-reduce.9.cloned.1.call-update) | async-done | bytes 1638416
  515.4 1.1 fusion.84
  516.5 1.1 fusion.82
  517.6 1.1 fusion.80
  518.7 1.1 fusion.78
  519.9 1.1 fusion.4
  521.0 1.1 fusion.7
  522.2 1.1 fusion.6
  523.3 1.3 multiply_reduce_fusion.1
  525.0 102.0 %psum.7 = f32[2,6000]{1,0:T(2,128)S(1)} all-reduce(f32[2,6000]{1,0:T(2,128)S(1)} %convolution_bitcast_fusion), channel_id=1, replica_groups=mesh['alt'=8,'strip'=64] {'alt','strip'}, use_global_device_ids=true, to_apply=%region_7.8 | all-reduce | flops 12000 | bytes 96000 | tf_op jit(solution)/shard_map/psum | solution.py:110
  627.8 0.7 pad_maximum_fusion.1
  (73 shorter events, 11.6 us)
Async XLA Ops:
  7.2 517.5 %copy-start = (bf16[2,25,6000]{2,0,1:T(2,128)(2,1)S(1)}, bf16[2,25,6000]{2,0,1:T(2,128)(2,1)}, u32[]{:S(2)}) copy-start(bf16[2,25,6000]{2,0,1:T(2,128)(2,1)} %param.12) | copy-start | bytes 1800004
  7.2 508.2 %all-reduce.9.cloned.1.call-start = ((), (), s32[]{:S(2)}) async-start(), calls=%async_computation | async-start | bytes 3276800
  33.6 1.7 copy-start.1
  37.9 477.5 %copy-start.3 = (f32[16,25]{1,0:T(8,128)S(1)}, f32[16,25]{1,0:T(8,128)}, u32[]{:S(2)}) copy-start(f32[16,25]{1,0:T(8,128)} %param.11) | copy-start | bytes 4804
  37.9 589.2 %copy-start.2 = (s32[6000]{0:T(1024)S(1)}, s32[6000]{0:T(1024)}, u32[]{:S(2)}) copy-start(s32[6000]{0:T(1024)} %param.13) | copy-start | bytes 72004
Sparse Core Ops, SparseCore 0:
  38.0 477.3 all-reduce.8
where the time goes:
time: 636 us; the launch traced here: 635 us
  waiting for transfers between devices  477 us (75%)
  blocking collectives  102 us (16%)
  local copies, waits for them, and re-layouts  20.2 us (3%)
  matrix products  16.4 us (3%)
  between operations  15.7 us (2%)
    unnamed x2, waiting for transfers between devices  477 us
    psum x1, blocking collectives, shards(): updates = lax.psum(partial_value, ('alt', 'strip'))  102 us
  transfers between devices with their start and end apart: 1, of which 1 were waited for; matrix products, arithmetic and copies ran while one was open for 0% of the time, Pallas kernels for 0%

commit v1 on v0

--- a/solution.py
+++ b/solution.py
@@ -107,7 +107,9 @@
         reconstructor.reshape(2 * count_here, ACTUATORS),
         preferred_element_type=jnp.float32,
     )
-    updates = lax.psum(partial_value, ("alt", "strip"))
+    updates = partial_value
+    for name in ("strip", "alt"):
+        updates = lax.psum(updates, name)
     limits = sat_code.astype(jnp.float32) * code_step
     first_cmd = jnp.clip(loop_gain * updates[0], -limits, limits)
     second_cmd = jnp.clip(first_cmd + loop_gain * updates[1], -limits, limits)

time: 636 us -> 781 us (1.23); the launches traced: 635 us -> 772 us
  blocking collectives: 102 us -> 238 us
    psum x1 -> x2, blocking collectives: 102 us -> 238 us  [shards(): updates = lax.psum(updates, name)]
where the time goes in v1:
time: 781 us; the launch traced here: 772 us
  waiting for transfers between devices  477 us (61%)
  blocking collectives  238 us (30%)
  local copies, waits for them, and re-layouts  20.2 us (3%)
  matrix products  16.4 us (2%)
  between operations  15.7 us (2%)
    unnamed x2, waiting for transfers between devices  477 us
    psum x2, blocking collectives, shards(): updates = lax.psum(updates, name)  238 us
  transfers between devices with their start and end apart: 1, of which 1 were waited for; matrix products, arithmetic and copies ran while one was open for 0% of the time, Pallas kernels for 0%

profile of v1, /device:TPU:1, one launch (start us, length us, event | category | flops | bytes accessed | tf_op | source)
XLA Modules:
  0.0 771.8 jit_solution(15213481787349528862)
XLA Ops:
  7.2 1.4 fusion.161
  10.0 0.7 fusion.159
  10.8 0.7 fusion.160
  11.8 0.7 slice_bitcast_fusion
  12.6 2.7 while.4
  13.2 0.7 bitcast_dynamic-update-slice_fusion.8
  14.6 0.7 bitcast_dynamic-update-slice_fusion.8
  15.5 2.5 while.5
  19.2 1.2 fusion.21
  20.5 1.2 fusion.1
  22.1 1.7 reshape.445
  24.2 2.7 while.6
  24.8 0.7 bitcast_dynamic-update-slice_fusion.10
  26.2 0.7 bitcast_dynamic-update-slice_fusion.10
  27.6 2.6 while.7
  28.2 0.7 bitcast_dynamic-update-slice_fusion.11
  29.5 0.7 bitcast_dynamic-update-slice_fusion.11
  30.8 1.2 fusion.18
  32.0 1.2 fusion
  33.7 1.7 reshape.448
  35.4 2.5 pad_maximum_fusion
  38.0 477.4 %all-reduce.9.cloned.1.call-done = f32[32,12800]{1,0:T(8,128)} async-done(((f32[32,12800]{1,0:T(8,128)}), f32[32,12800]{1,0:T(8,128)}) %all-reduce.9.cloned.1.call-update) | async-done | bytes 1638416
  515.4 1.1 fusion.84
  516.5 1.1 fusion.82
  517.6 1.1 fusion.80
  518.7 1.1 fusion.78
  519.9 1.1 fusion.4
  521.0 1.1 fusion.7
  522.2 1.1 fusion.6
  523.3 1.3 multiply_reduce_fusion.1
  525.0 205.0 %psum.14 = f32[2,6000]{1,0:T(2,128)S(1)} all-reduce(f32[2,6000]{1,0:T(2,128)S(1)} %convolution_bitcast_fusion), channel_id=1, replica_groups=mesh['alt'=8,'strip'=64] {'strip'}, use_global_device_ids=true, to_apply=%region_7.8 | all-reduce | flops 12000 | bytes 96000 | tf_op jit(solution)/shard_map/psum | solution.py:112
  730.0 33.5 %psum.15 = f32[2,6000]{1,0:T(2,128)S(1)} all-reduce(f32[2,6000]{1,0:T(2,128)S(1)} %psum.14), channel_id=1, replica_groups=mesh['alt'=8,'strip'=64] {'alt'}, use_global_device_ids=true, to_apply=%region_8.9 | all-reduce | flops 12000 | bytes 96000 | tf_op jit(solution)/shard_map/psum | solution.py:112
  (74 shorter events, 12.3 us)
Async XLA Ops:
  7.2 517.5 %copy-start = (bf16[2,25,6000]{2,0,1:T(2,128)(2,1)S(1)}, bf16[2,25,6000]{2,0,1:T(2,128)(2,1)}, u32[]{:S(2)}) copy-start(bf16[2,25,6000]{2,0,1:T(2,128)(2,1)} %param.12) | copy-start | bytes 1800004
  7.2 508.2 %all-reduce.9.cloned.1.call-start = ((), (), s32[]{:S(2)}) async-start(), calls=%async_computation | async-start | bytes 3276800
  33.6 1.7 copy-start.1
  37.9 477.5 %copy-start.3 = (f32[16,25]{1,0:T(8,128)S(1)}, f32[16,25]{1,0:T(8,128)}, u32[]{:S(2)}) copy-start(f32[16,25]{1,0:T(8,128)} %param.11) | copy-start | bytes 4804
  37.9 725.7 %copy-start.2 = (s32[6000]{0:T(1024)S(1)}, s32[6000]{0:T(1024)}, u32[]{:S(2)}) copy-start(s32[6000]{0:T(1024)} %param.13) | copy-start | bytes 72004
Sparse Core Ops, SparseCore 0:
  38.0 477.3 all-reduce.8
